TPU v7x, 512 devices: a whole 4x4x16 slice. The times are simulated.
512 devices in a mesh: rcv: 64 (over y_lo, z, core), seg: 8 (over x, y_hi).
Axes of the slice: x: 4, y: 4 (y_hi: 2, y_lo: 2; y = y_hi * 2 + y_lo), z: 16, core: 2. Of those that a mesh axis runs over, the one named last changes fastest.
Arguments:
- traces: bfloat16 [1024, 32, 1500], P('rcv', 'seg'), may hold values from -6 to 6
- panel_start: int32 [2], replicated, may hold values from 0 to 896
- valid: int32 [32], P('seg'), may hold values 0 or 1
Outputs:
- stack: float32 [2, 128, 1024, 256], P(None, 'seg', 'rcv')
All inputs are finite; a program needn't handle non-finite values. No bound on the sum of `valid` on one device may be relied on, other than what follows from the above.
Results may differ from a plain program's by a relative error of at most 0.0049.
Values may be sent and summed in bfloat16 or wider, within the bound.
A program may use at most 128 MiB of HBM per device.

v0:
```python
import math

import jax
import jax.numpy as jnp
from jax import lax
from jax.sharding import PartitionSpec as P

PANELS = 2
SRC = 128
NFFT = 1664
K0 = 3
F = 320
LAG = 128


def forward_table(samples, bins, first, length):
    times = jnp.arange(samples, dtype=jnp.int32)
    freqs = first + jnp.arange(bins, dtype=jnp.int32)
    phase = jnp.mod(times[:, None] * freqs[None, :], length).astype(jnp.float32)
    angle = 2.0 * math.pi / length * phase
    return jnp.concatenate([jnp.cos(angle), -jnp.sin(angle)], axis=1).astype(jnp.bfloat16)


def inverse_table(bins, first, length, half_lag):
    freqs = first + jnp.arange(bins, dtype=jnp.int32)
    delays = jnp.arange(2 * half_lag, dtype=jnp.int32) - half_lag
    phase = jnp.mod(freqs[:, None] * delays[None, :], length).astype(jnp.float32)
    angle = 2.0 * math.pi / length * phase
    scale = 1.0 / math.sqrt(bins)
    return jnp.concatenate([jnp.cos(angle), -jnp.sin(angle)], axis=0) * scale


def whiten(spec, bins):
    real_part = spec[:, :bins]
    imag_part = spec[:, bins:]
    power = real_part * real_part + imag_part * imag_part
    level = jnp.mean(power, axis=1, keepdims=True) + 1e-06
    factor = lax.rsqrt(power + 0.1 * level)
    return (spec * jnp.concatenate([factor, factor], axis=1)).astype(jnp.bfloat16)


def correlate(sources, receivers, flags, norm):
    highest = lax.Precision.HIGHEST
    masked = sources * flags[None, None, :, None]
    src_re, src_im = (masked[..., :F], masked[..., F:])
    rcv_re, rcv_im = (receivers[..., :F], receivers[..., F:])
    cross_re = jnp.einsum(
        "psgk,bgk->psbk", src_re, rcv_re, preferred_element_type=jnp.float32
    ) + jnp.einsum("psgk,bgk->psbk", src_im, rcv_im, preferred_element_type=jnp.float32)
    cross_im = jnp.einsum(
        "psgk,bgk->psbk", src_re, rcv_im, preferred_element_type=jnp.float32
    ) - jnp.einsum("psgk,bgk->psbk", src_im, rcv_re, preferred_element_type=jnp.float32)
    cross = jnp.concatenate([cross_re, cross_im], axis=3) * norm
    return jnp.einsum("psbk,kl->psbl", cross, inverse_table(F, K0, NFFT, LAG), precision=highest)


def body(traces, panel_start, valid):
    rows, segs, samples = traces.shape
    table = forward_table(samples, F, K0, NFFT)
    spec = jnp.dot(traces.reshape(rows * segs, samples), table, preferred_element_type=jnp.float32)
    white = whiten(spec, F).reshape(rows, segs, 2 * F)
    picks = panel_start[:, None] + jnp.arange(SRC, dtype=jnp.int32)[None, :]
    total_segs = segs * lax.axis_size("seg")
    norm = 1.0 / math.sqrt(total_segs)
    piece = lax.all_gather(white, "rcv", axis=0, tiled=True)
    count = piece.shape[0]
    members = jnp.arange(count, dtype=jnp.int32)
    onehot = (picks[:, :, None] == members[None, None, :]).astype(jnp.bfloat16)
    chosen = jnp.dot(
        onehot.reshape(PANELS * SRC, count),
        piece.reshape(count, segs * 2 * F),
        preferred_element_type=jnp.float32,
    )
    gathered = chosen.reshape(PANELS, SRC, segs, 2 * F)
    sources = gathered.astype(jnp.bfloat16)
    flags = valid.astype(jnp.bfloat16)
    partial_lags = correlate(sources, white, flags, norm)
    return lax.psum_scatter(partial_lags, "seg", scatter_dimension=1, tiled=True)


def solution(mesh):
    return jax.shard_map(
        body,
        mesh=mesh,
        in_specs=(P("rcv", "seg", None), P(), P("seg")),
        out_specs=P(None, "seg", "rcv", None),
        check_vma=False,
    )
```

profile of v0, /device:TPU:1, one launch (start us, length us, event | category | flops | bytes accessed | tf_op | source)
XLA Modules:
  0.0 328.8 jit_solution(11109025334540206131)
XLA Ops:
  6.5 9.9 %cosine_convert_fusion = (bf16[1500,320]{1,0:T(8,128)(2,1)S(1)}, bf16[1500,320]{1,0:T(8,128)(2,1)S(1)}) fusion(s32[320]{0:T(512)S(1)} %iota_add_fusion), kind=kLoop, calls=%fused_computation.13 | loop fusion | flops 5760000 | bytes 1921280 | tf_op jit(solution)/shard_map/convert
  16.4 1.0 reshape.78
  17.4 0.7 fusion.21
  18.5 0.7 reshape.79
  19.3 1.0 slice_bitcast_fusion.1
  20.8 2.2 fusion.36
  23.1 128.0 %all-gather.2.cloned.1.call-done = bf16[1024,4,640]{2,1,0:T(4,128)(2,1)} async-done(((bf16[16,4,640]{2,1,0:T(4,128)(2,1)}), bf16[1024,4,640]{2,1,0:T(4,128)(2,1)}) %all-gather.2.cloned.1.call-update) | async-done | bytes 5242896 | tf_op jit(solution)/shard_map/all_gather | solution.py:65
  151.0 9.1 %copy.18 = bf16[1024,4,640]{0,2,1:T(8,128)(2,1)} copy(bf16[1024,4,640]{2,1,0:T(4,128)(2,1)} %all-gather.2.cloned.1.call-done) | data formatting | bytes 10485760 | tf_op jit(solution)/shard_map/reshape | solution.py:71
  160.1 4.1 %fusion.18 = bf16[2,128,4,640]{3,1,2,0:T(8,128)(2,1)S(1)} fusion(bf16[1024,4,640]{0,2,1:T(8,128)(2,1)} %copy.18, bf16[4]{0:T(256)(128)(2,1)S(1)} %convert_element_type.24, s32[2,128]{1,0:T(2,128)S(1)} %iota_add_fusion.2), kind=kOutput, calls=%fused_computation.23 | convolution fusion | flops 1343750144 | bytes 6554632 | tf_op jit(solution)/shard_map/dot_general | solution.py:69
  164.2 0.4 fusion.45
  164.6 0.7 copy.10
  165.3 0.7 copy.13
  166.0 3.0 fusion.46
  169.0 2.9 fusion.49
  171.9 2.8 fusion.47
  174.7 3.0 fusion.48
  177.6 6.3 %copy.11 = f32[320,16,2,128]{0,3,1,2:T(8,128)} copy(f32[320,16,2,128]{3,1,2,0:T(8,128)} %fusion.46) | data formatting | bytes 10485760 | tf_op jit(solution)/shard_map/psgk,bgk->psbk/dot_general | solution.py:47
  184.0 6.3 %copy.14 = f32[320,16,2,128]{0,3,1,2:T(8,128)} copy(f32[320,16,2,128]{3,1,2,0:T(8,128)} %fusion.47) | data formatting | bytes 10485760 | tf_op jit(solution)/shard_map/psgk,bgk->psbk/dot_general | solution.py:49
  190.3 6.3 %copy.16 = f32[320,16,2,128]{0,3,1,2:T(8,128)} copy(f32[320,16,2,128]{3,1,2,0:T(8,128)} %fusion.49) | data formatting | bytes 10485760 | tf_op jit(solution)/shard_map/psgk,bgk->psbk/dot_general | solution.py:52
  196.7 6.3 %copy.15 = f32[320,16,2,128]{0,3,1,2:T(8,128)} copy(f32[320,16,2,128]{3,1,2,0:T(8,128)} %fusion.48) | data formatting | bytes 10485760 | tf_op jit(solution)/shard_map/psgk,bgk->psbk/dot_general | solution.py:50
  203.0 9.1 %subtract_bitcast_fusion = (f32[2,128,16,320]{3,1,2,0:T(8,128)S(1)}, f32[2,128,16,320]{3,1,2,0:T(8,128)S(1)}) fusion(f32[320,16,2,128]{0,3,1,2:T(8,128)} %copy.15, f32[320,16,2,128]{0,3,1,2:T(8,128)} %copy.16, f32[320,16,2,128]{0,3,1,2:T(8,128)} %copy.11, f32[320,16,2,128]{0,3,1,2:T(8,128)} %copy.14), kind=kLoop, calls=%fused_computation.4 | loop fusion | flops 2621440 | bytes 31457280 | tf_op jit(solution)/shard_map/sub | solution.py:50
  212.1 12.7 %fusion = f32[2,128,16,256]{3,1,2,0:T(8,128)} fusion(f32[2,128,16,320]{3,1,2,0:T(8,128)S(1)} %get-tuple-element.13, f32[2,128,16,320]{3,1,2,0:T(8,128)S(1)} %get-tuple-element.14, f32[320,256]{1,0:T(8,128)S(1)} %copy-done.1, f32[320,256]{1,0:T(8,128)S(1)} %copy-done), kind=kOutput, calls=%fused_computation.1 | convolution fusion | flops 8058634240 | bytes 15335424 | tf_op jit(solution)/shard_map/psbk,kl->psbl/dot_general | solution.py:54
  224.8 95.0 %reduce-scatter.2.cloned.1.call-done = f32[2,16,16,256]{3,1,2,0:T(8,128)} async-done(((f32[2,128,16,256]{3,1,2,0:T(8,128)}), f32[2,16,16,256]{3,1,2,0:T(8,128)}) %reduce-scatter.2.cloned.1.call-update) | async-done | bytes 524304 | tf_op jit(solution)/shard_map/reduce_scatter | solution.py:78
  319.8 2.1 copy.7
  (22 shorter events, 1.1 us)
Async XLA Ops:
  6.5 144.5 %all-gather.2.cloned.1.call-start = ((), (), s32[]{:S(2)}) async-start(), calls=%async_computation.1 | async-start | bytes 5324800 | tf_op jit(solution)/shard_map/all_gather | solution.py:65
  16.4 2.9 copy-start.2
  16.4 4.3 %copy-start.3 = (s32[2]{0:T(128)S(1)}, s32[2]{0:T(128)}, u32[]{:S(2)}) copy-start(s32[2]{0:T(128)} %param.4) | copy-start | bytes 28
  19.2 300.6 %reduce-scatter.2.cloned.1.call-start = ((), (), s32[]{:S(2)}) async-start(), calls=%async_computation.2 | async-start | bytes 4718592 | tf_op jit(solution)/shard_map/reduce_scatter | solution.py:78
  203.0 9.1 %copy-start = (f32[320,256]{1,0:T(8,128)S(1)}, f32[320,256]{1,0:T(8,128)}, u32[]{:S(2)}) copy-start(f32[320,256]{1,0:T(8,128)} %get-tuple-element.9) | copy-start | bytes 983044
  203.0 9.1 %copy-start.1 = (f32[320,256]{1,0:T(8,128)S(1)}, f32[320,256]{1,0:T(8,128)}, u32[]{:S(2)}) copy-start(f32[320,256]{1,0:T(8,128)} %get-tuple-element.10) | copy-start | bytes 983044
Sparse Core Ops, SparseCore 0:
  19.3 131.6 all-gather.1
  224.9 94.8 reduce-scatter.1
where the time goes:
time: 330 us; the launch traced here: 329 us
  waiting for transfers between devices  223 us (68%)
  local copies, waits for them, and re-layouts  41.6 us (13%)
  matrix products  29 us (9%)
  other arithmetic  21.6 us (7%)
  between operations  13.6 us (4%)
    all_gather x1, waiting for transfers between devices, body(): piece = lax.all_gather(white, 'rcv', axis=0, tiled=True)  128 us
    reduce_scatter x1, waiting for transfers between devices, body(): lax.psum_scatter(partial_lags, 'seg', scatter_dimension=1, tiled=True)  95 us
    dot_general x1, matrix products, correlate(): jnp.einsum('psbk,kl->psbl', cross, inverse_table(F, K0, NFFT, LAG), preci...  12.7 us
    another operation x1, other arithmetic  9.85 us
    reshape x1, local copies, waits for them, and re-layouts, body(): piece.reshape(count, segs * 2 * F)  9.08 us
    sub x1, other arithmetic, correlate(): jnp.einsum('psgk,bgk->psbk', src_re, rcv_im, preferred_element_type=jnp.f...  9.05 us
  transfers between devices with their start and end apart: 2, of which 2 were waited for; matrix products, arithmetic and copies ran while one was open for 1% of the time, Pallas kernels for 0%

commit v1 on v0

v1 whole, which is shorter than its diff:
```python
import functools
import math

import jax
import jax.numpy as jnp
import ml_dtypes
import numpy as np
from jax import lax
from jax.experimental import pallas as pl
from jax.experimental.pallas import tpu as pltpu
from jax.sharding import PartitionSpec as P

PANELS = 2
SRC = 128
NFFT = 1664
K0 = 3
F = 320
LAG = 128
SEGS = 32
Z = 16
C = 2 * F
KPAD = 1536
W = 768
MESH = pl.DeviceIdType.MESH


def column_order():
    re = np.arange(F)
    im = F + np.arange(F)
    return np.concatenate(
        [re[:128], im[:128], re[128:256], im[128:256], re[256:], im[256:]]
    )


def forward_table(samples):
    times = np.arange(samples, dtype=np.int64)
    freqs = K0 + np.arange(F, dtype=np.int64)
    phase = np.mod(times[:, None] * freqs[None, :], NFFT)
    angle = 2.0 * math.pi / NFFT * phase
    table = np.concatenate([np.cos(angle), -np.sin(angle)], axis=1)[:, column_order()]
    full = np.zeros((KPAD, C), np.float32)
    full[:samples] = table
    return full.astype(ml_dtypes.bfloat16)


def inverse_table(total_segs):
    freqs = K0 + np.arange(F, dtype=np.int64)
    delays = np.arange(2 * LAG, dtype=np.int64) - LAG
    phase = np.mod(freqs[:, None] * delays[None, :], NFFT)
    angle = 2.0 * math.pi / NFFT * phase
    scale = 1.0 / math.sqrt(F) / math.sqrt(total_segs)
    cos = np.cos(angle) * scale
    sin = np.sin(angle) * scale
    rows = [cos[:128], -sin[:128], cos[128:256], -sin[128:256]]
    rows += [cos[256:], cos[256:], -sin[256:], sin[256:]]
    return np.concatenate(rows, axis=0).astype(np.float32).astype(ml_dtypes.bfloat16)


def kernel(
    start_ref, valid_ref, tr_ref, tab_hbm, inv_hbm, out_ref,
    tab, inv, white, c1, p1, c2, src, rcv, rcvf, srcf, acc, xb,
    tab_sem, l1_send, l1_recv, l2_send, l2_recv, rc_send, rc_recv,
    ga_send, ga_recv, ring_send, ring_recv, sib_send, sib_recv,
):
    R = lax.axis_index("rcv")
    S = lax.axis_index("seg")
    yl = R // 32
    z = (R // 2) % Z
    core = R % 2
    m = R // 8
    w = R % 8
    diagonal = w == S

    def dev(yl_, z_, core_):
        return yl_ * 32 + z_ * 2 + core_

    zright = lax.rem(z + 1, Z)
    zleft = lax.rem(z + Z - 1, Z)
    sibling = dev(yl, z, 1 - core)

    tab_copies = []
    for i in range(3):
        rows = pl.ds(512 * i, 512)
        cp = pltpu.make_async_copy(tab_hbm.at[rows], tab.at[rows], tab_sem.at[i])
        cp.start()
        tab_copies.append(cp)
    inv_copy = pltpu.make_async_copy(inv_hbm, inv, tab_sem.at[3])
    inv_copy.start()

    barrier = pltpu.get_barrier_semaphore()

    def greet(r, s):
        pl.semaphore_signal(barrier, inc=1, device_id=(r, s), device_id_type=MESH)

    for d in range(1, 8):
        greet(lax.rem(m + d, 8) * 8 + w, S)
        greet(R, lax.rem(S + d, 8))
        greet(m * 8 + lax.rem(w + d, 8), w)

    @pl.when(jnp.logical_not(diagonal))
    def _():
        greet(R, w)

    for a, b in ((0, 1), (1, 0), (1, 1)):
        greet(dev(yl ^ a, z, core ^ b), S)
    greet(dev(yl, zright, core), S)
    greet(dev(yl, zleft, core), S)

    spec = None
    for i in range(3):
        tab_copies[i].wait()
        part = jnp.dot(
            tr_ref[:, pl.ds(512 * i, 512)],
            tab[pl.ds(512 * i, 512), :],
            preferred_element_type=jnp.float32,
        )
        spec = part if spec is None else spec + part
    sq = spec * spec
    pa = sq[:, 0:128] + sq[:, 128:256]
    pb = sq[:, 256:384] + sq[:, 384:512]
    pe = sq[:, 512:640]
    level = jnp.sum(pa + pb + pe, axis=1, keepdims=True) * (1.0 / F) + 1e-06
    level = 0.1 * level
    pe = pe + pltpu.roll(pe, 64, 1)
    rows = lax.broadcasted_iota(jnp.int32, (64, 1), 0) // 16
    flag = jnp.zeros((64, 1), jnp.float32)
    for g in range(4):
        flag = jnp.where(rows == g, valid_ref[g].astype(jnp.float32), flag)
    fa = lax.rsqrt(pa + level)
    fb = lax.rsqrt(pb + level)
    fe = lax.rsqrt(pe + level)
    factor = jnp.concatenate([fa, fa, fb, fb, fe], axis=1)
    whitened = (spec * factor * flag).astype(jnp.bfloat16)
    for b in range(8):
        white[b] = whitened[8 * b : 8 * b + 8]

    pl.semaphore_wait(barrier, jnp.where(diagonal, 26, 27))

    l1 = []
    for d in range(1, 8):
        other = lax.rem(m + d, 8)
        cp = pltpu.make_async_remote_copy(
            src_ref=white.at[other], dst_ref=c1.at[m],
            send_sem=l1_send.at[d], recv_sem=l1_recv.at[d],
            device_id=(other * 8 + w, S), device_id_type=MESH,
        )
        cp.start()
        l1.append(cp)
    c1[m] = white[m]

    rc = []
    for d in range(1, 8):
        cp = pltpu.make_async_remote_copy(
            src_ref=white, dst_ref=rcv.at[S],
            send_sem=rc_send.at[d], recv_sem=rc_recv.at[d],
            device_id=(R, lax.rem(S + d, 8)), device_id_type=MESH,
        )
        cp.start()
        rc.append(cp)
    rcv[S] = white[...]
    acc[...] = jnp.zeros_like(acc)

    for cp in l1:
        cp.wait_recv()
    v = lax.broadcasted_iota(jnp.int32, (8, 1), 0) + 8 * (m % 2)
    cand = [c1[mm].astype(jnp.float32) for mm in range(8)]
    for p in range(PANELS):
        st = start_ref[p]
        pick = jnp.zeros((8, C), jnp.float32)
        for mm in range(8):
            j = 128 * mm + 16 * w + v - st
            pick = jnp.where((j >= 0) & (j < SRC), cand[mm], pick)
        p1[p] = pick.astype(jnp.bfloat16)

    l2 = []
    for d in range(8):
        cp = pltpu.make_async_remote_copy(
            src_ref=p1, dst_ref=c2.at[w],
            send_sem=l2_send.at[d], recv_sem=l2_recv.at[w],
            device_id=(m * 8 + S, lax.rem(S + d, 8)), device_id_type=MESH,
        )
        l2.append(cp)
        if d == 0:
            pl.when(jnp.logical_not(diagonal))(cp.start)
        else:
            cp.start()

    @pl.when(diagonal)
    def _():
        c2[w] = p1[...]

    for ww in range(8):
        cp = pltpu.make_async_remote_copy(
            src_ref=p1, dst_ref=c2.at[ww],
            send_sem=l2_send.at[0], recv_sem=l2_recv.at[ww],
            device_id=(m * 8 + S, S), device_id_type=MESH,
        )
        pl.when(jnp.logical_not(diagonal & (w == ww)))(cp.wait_recv)

    for p in range(PANELS):
        st = start_ref[p]
        pick = jnp.zeros((8, C), jnp.float32)
        for ww in range(8):
            j = (16 * ww + v - st) & (SRC - 1)
            pick = jnp.where((j >> 4) == S, c2[ww, p].astype(jnp.float32), pick)
        src[z, yl, core, p] = pick.astype(jnp.bfloat16)

    ga = []
    for i, (a, b) in enumerate(((0, 1), (1, 0), (1, 1))):
        cp = pltpu.make_async_remote_copy(
            src_ref=src.at[z, yl, core], dst_ref=src.at[z, yl, core],
            send_sem=ga_send.at[i], recv_sem=ga_recv.at[i],
            device_id=(dev(yl ^ a, z, core ^ b), S), device_id_type=MESH,
        )
        cp.start()
        ga.append(cp)
    for cp in ga:
        cp.wait_recv()

    def ring(way, k, ref):
        return pltpu.make_async_remote_copy(
            src_ref=ref, dst_ref=ref,
            send_sem=ring_send.at[way, k], recv_sem=ring_recv.at[way, k],
            device_id=(dev(yl, zright if way == 0 else zleft, core), S),
            device_id_type=MESH,
        )

    def across(way, k, ref):
        return pltpu.make_async_remote_copy(
            src_ref=ref, dst_ref=ref,
            send_sem=sib_send.at[way, k], recv_sem=sib_recv.at[way, k],
            device_id=(sibling, S), device_id_type=MESH,
        )

    def at(way, k):
        return lax.rem(z + (Z - k if way == 0 else k), Z)

    def chunk(zc):
        zq = zc // 4
        vbase = (zq % 2) * 8
        sbase = (zc % 4) * 8 + zq // 2
        for pc in range(4):
            for p in range(PANELS):
                srcf[pc, p] = src[zc, pc // 2, pc % 2, p].astype(jnp.float32)

        def panel(p, carry):
            for vg in range(2):
                for t in range(3):
                    lanes = [pl.ds(256 * t, 128), pl.ds(256 * t + 128, 128)]
                    sums = [
                        [
                            [acc[p, vbase + vg * 4 + i, half, :, ln] for ln in lanes]
                            for half in range(2)
                        ]
                        for i in range(4)
                    ]
                    for pc in range(4):
                        seg = sbase + 4 * (pc % 2) + 2 * (pc // 2)
                        got = [
                            [rcvf[seg, half, :, ln] for ln in lanes] for half in range(2)
                        ]
                        for i in range(4):
                            row = pl.ds(vg * 4 + i, 1)
                            s0 = srcf[pc, p, row, lanes[0]]
                            if t < 2:
                                s1 = srcf[pc, p, row, lanes[1]]
                            for half in range(2):
                                r0, r1 = got[half]
                                here = sums[i][half]
                                if t < 2:
                                    here[0] = here[0] + s0 * r0 + s1 * r1
                                    here[1] = here[1] + s0 * r1 - s1 * r0
                                else:
                                    here[0] = here[0] + s0 * r0
                                    here[1] = here[1] + s0 * r1
                    for i in range(4):
                        for half in range(2):
                            for n in range(2):
                                acc[p, vbase + vg * 4 + i, half, :, lanes[n]] = sums[i][
                                    half
                                ][n]
            return carry

        lax.fori_loop(0, PANELS, panel, 0)

    for way in range(2):
        ring(way, 1, src.at[z, core]).start()

    for cp in rc:
        cp.wait_recv()

    def widen(sp, carry):
        for b in range(8):
            block = rcv[sp, b].astype(jnp.float32)
            rcvf[sp * 4 + b // 2, b % 2, :, pl.ds(0, C)] = block
            rcvf[sp * 4 + b // 2, b % 2, :, pl.ds(C, 128)] = pltpu.roll(
                block[:, 512:640], 64, 1
            )
        return carry

    lax.fori_loop(0, 8, widen, 0)
    chunk(z)

    def step(k, carry):
        for way in range(2):
            ring(way, k, src.at[at(way, k), core]).wait_recv()
        for way in range(2):
            ring(way, k + 1, src.at[at(way, k), core]).start()
        for way in range(2):
            across(way, k, src.at[at(way, k), core]).start()
        for way in range(2):
            across(way, k, src.at[at(way, k), core]).wait_recv()
        for way in range(2):
            chunk(at(way, k))
        return carry

    lax.fori_loop(1, 7, step, 0)
    last = lax.rem(z + 8, Z)
    for way in range(2):
        ring(way, 7, src.at[at(way, 7), core]).wait_recv()
    for way in range(2):
        ring(way, 8, src.at[at(way, 7), core, way]).start()
    for way in range(2):
        across(way, 7, src.at[at(way, 7), core]).start()
    for way in range(2):
        across(way, 7, src.at[at(way, 7), core]).wait_recv()
    for way in range(2):
        chunk(at(way, 7))
    for way in range(2):
        ring(way, 8, src.at[last, core, way]).wait_recv()
        across(way, 8, src.at[last, core, way]).start()
    for way in range(2):
        across(way, 8, src.at[last, core, way]).wait_recv()
    chunk(last)

    inv_copy.wait()
    for p in range(PANELS):
        st = start_ref[p]
        for i in range(16):
            xb[pl.ds(16 * i, 16)] = (
                acc[p, (st + i) & 15].reshape(16, W).astype(jnp.bfloat16)
            )
        out_ref[p] = jnp.dot(
            xb[...], inv[...], preferred_element_type=jnp.float32
        )

    for cp in l1 + rc + ga + l2[1:]:
        cp.wait_send()
    pl.when(jnp.logical_not(diagonal))(l2[0].wait_send)

    def drain(k, carry):
        for way in range(2):
            ring(way, k, src.at[z, core]).wait_send()
            across(way, k, src.at[z, core]).wait_send()
        return carry

    lax.fori_loop(1, 8, drain, 0)
    for way in range(2):
        ring(way, 8, src.at[z, core, way]).wait_send()
        across(way, 8, src.at[z, core, way]).wait_send()


def body(traces, panel_start, valid):
    rows, segs, samples = traces.shape
    table = jnp.asarray(forward_table(samples))
    inv = jnp.asarray(inverse_table(segs * lax.axis_size("seg")))
    tr = jnp.transpose(traces, (1, 0, 2)).reshape(segs * rows, samples)
    tr = jnp.pad(tr, ((0, 0), (0, KPAD - samples)))
    bf = jnp.bfloat16
    f32 = jnp.float32
    dma = pltpu.SemaphoreType.DMA
    out = pl.pallas_call(
        kernel,
        out_shape=jax.ShapeDtypeStruct((PANELS, 256, 2 * LAG), f32),
        in_specs=[
            pl.BlockSpec(memory_space=pltpu.SMEM),
            pl.BlockSpec(memory_space=pltpu.SMEM),
            pl.BlockSpec(memory_space=pltpu.VMEM),
            pl.BlockSpec(memory_space=pl.ANY),
            pl.BlockSpec(memory_space=pl.ANY),
        ],
        out_specs=pl.BlockSpec(memory_space=pltpu.VMEM),
        scratch_shapes=[
            pltpu.VMEM((KPAD, C), bf),
            pltpu.VMEM((W, 2 * LAG), bf),
            pltpu.VMEM((8, 8, C), bf),
            pltpu.VMEM((8, 8, C), bf),
            pltpu.VMEM((2, 8, C), bf),
            pltpu.VMEM((8, 2, 8, C), bf),
            pltpu.VMEM((Z, 2, 2, 2, 8, C), bf),
            pltpu.VMEM((8, 8, 8, C), bf),
            pltpu.VMEM((SEGS, 2, 8, W), f32),
            pltpu.VMEM((4, 2, 8, C), f32),
            pltpu.VMEM((2, 16, 2, 8, W), f32),
            pltpu.VMEM((256, W), bf),
            dma((4,)),
            dma((8,)), dma((8,)), dma((8,)), dma((8,)), dma((8,)), dma((8,)),
            dma((3,)), dma((3,)), dma((2, 9)), dma((2, 9)), dma((2, 9)), dma((2, 9)),
        ],
        compiler_params=pltpu.CompilerParams(
            collective_id=0, has_side_effects=True, vmem_limit_bytes=60 * 1024 * 1024
        ),
    )(panel_start, valid, tr, table, inv)
    return out.reshape(PANELS, 16, 16, 2 * LAG)


def solution(mesh):
    return jax.shard_map(
        body,
        mesh=mesh,
        in_specs=(P("rcv", "seg", None), P(), P("seg")),
        out_specs=P(None, "seg", "rcv", None),
        check_vma=False,
    )
```

time: 330 us -> 75.4 us (0.23)
  waiting for transfers between devices: 223 us -> 0 us
  Pallas kernels: 0 us -> 71.6 us
  local copies, waits for them, and re-layouts: 41.6 us -> 3.53 us
  matrix products: 29 us -> 0 us
  other arithmetic: 21.6 us -> 0 us
  between operations: 13.6 us -> 0.01 us
    all_gather x1 -> x0, waiting for transfers between devices: 128 us -> none  [body(): piece = lax.all_gather(white, 'rcv', axis=0, tiled=True)]
    reduce_scatter x1 -> x0, waiting for transfers between devices: 95 us -> none  [body(): lax.psum_scatter(partial_lags, 'seg', scatter_dimension=1, tiled=True)]
    pallas_call x0 -> x1, Pallas kernels: none -> 71.6 us  [body(): pl.pallas_call(kernel, out_shape=jax.ShapeDtypeStruct((PANELS, 256, 2 * L...]
    dot_general x7 -> x0, matrix products: 29 us -> none  [the longest x1 12.7 us: correlate(): jnp.einsum('psbk,kl->psbl', cross, inverse_table(F, K0, NFFT, LAG), preci...]
    dot_general x4 -> x0, local copies, waits for them, and re-layouts: 25.4 us -> none  [the longest x1 6.35 us: correlate(): jnp.einsum('psgk,bgk->psbk', src_im, rcv_re, preferred_element_type=jnp.f...]
    reshape x3 -> x0, local copies, waits for them, and re-layouts: 10.7 us -> none  [the longest x1 9.08 us: body(): piece.reshape(count, segs * 2 * F)]
    another operation x1 -> x0, other arithmetic: 9.85 us -> none
    sub x2 -> x0, other arithmetic: 9.06 us -> none  [the longest x1 9.05 us: correlate(): jnp.einsum('psgk,bgk->psbk', src_re, rcv_im, preferred_element_type=jnp.f...]
  transfers between devices with their start and end apart: 2 -> 0, of which waited for: 2 -> 0; matrix products, arithmetic and copies ran while one was open for 1% -> 0% of each run, Pallas kernels for 0% -> 0%
where the time goes in v1:
time: 75.4 us; the launch traced here: 75.2 us
  Pallas kernels  71.6 us (95%)
  local copies, waits for them, and re-layouts  3.53 us (5%)
    pallas_call x1, Pallas kernels, body(): pl.pallas_call(kernel, out_shape=jax.ShapeDtypeStruct((PANELS, 256, 2 * L...  71.6 us
    unnamed x1, local copies, waits for them, and re-layouts  1.87 us

profile of v1, /device:TPU:1, one launch (start us, length us, event | category | flops | bytes accessed | tf_op | source)
XLA Modules:
  0.0 75.2 jit_solution(18056367186985123628)
XLA Ops:
  0.0 1.0 %copy.6 = bf16[4,16,1500]{2,1,0:T(8,128)(2,1)S(1)} copy(bf16[4,16,1500]{2,0,1:T(4,128)(2,1)} %bitcast.5) | data formatting | bytes 384000 | tf_op jit(solution)/shard_map/transpose | solution.py:367
  1.0 0.7 pad.4.tr_ref
  1.7 71.6 %shard_map.55 = f32[2,256,256]{2,1,0:T(8,128)} custom-call(s32[2]{0:T(128)} %start_ref.1, s32[4]{0:T(128)} %valid_ref.1, bf16[64,1536]{1,0:T(8,128)(2,1)} %pad.4.tr_ref, bf16[1536,640]{1,0:T(8,128)(2,1)} %constant.7.clone.tab_hbm, bf16[768,256]{1,0:T(8,128)(2,1)} %constant.8.clone.inv_hbm), custom_call_target="tpu_custom_call" | custom-call | tf_op jit(solution)/shard_map/pallas_call | solution.py:372
  73.3 1.9 %copy.8 = f32[2,16,16,256]{3,2,1,0:T(8,128)} copy(f32[2,16,16,256]{3,2,1,0:T(8,128)} %bitcast.3) | data formatting | bytes 1048576

commit v2 on v1

v2 whole, which is shorter than its diff:
```python
import functools
import math

import jax
import jax.numpy as jnp
import ml_dtypes
import numpy as np
from jax import lax
from jax.experimental import pallas as pl
from jax.experimental.pallas import tpu as pltpu
from jax.sharding import PartitionSpec as P

PANELS = 2
SRC = 128
NFFT = 1664
K0 = 3
F = 320
LAG = 128
SEGS = 32
Z = 16
C = 2 * F
KPAD = 1536
W = 768
MESH = pl.DeviceIdType.MESH


def column_order():
    re = np.arange(F)
    im = F + np.arange(F)
    return np.concatenate(
        [re[:128], im[:128], re[128:256], im[128:256], re[256:], im[256:]]
    )


def forward_table(samples):
    times = np.arange(samples, dtype=np.int64)
    freqs = K0 + np.arange(F, dtype=np.int64)
    phase = np.mod(times[:, None] * freqs[None, :], NFFT)
    angle = 2.0 * math.pi / NFFT * phase
    table = np.concatenate([np.cos(angle), -np.sin(angle)], axis=1)[:, column_order()]
    full = np.zeros((KPAD, C), np.float32)
    full[:samples] = table
    return full.astype(ml_dtypes.bfloat16)


def inverse_table(total_segs):
    freqs = K0 + np.arange(F, dtype=np.int64)
    delays = np.arange(2 * LAG, dtype=np.int64) - LAG
    phase = np.mod(freqs[:, None] * delays[None, :], NFFT)
    angle = 2.0 * math.pi / NFFT * phase
    scale = 1.0 / math.sqrt(F) / math.sqrt(total_segs)
    cos = np.cos(angle) * scale
    sin = np.sin(angle) * scale
    rows = [cos[:128], -sin[:128], cos[128:256], -sin[128:256]]
    rows += [cos[256:], cos[256:], -sin[256:], sin[256:]]
    return np.concatenate(rows, axis=0).astype(np.float32).astype(ml_dtypes.bfloat16)


def kernel(
    start_ref, valid_ref, tr_ref, tab_hbm, inv_hbm, out_ref,
    tab, inv, white, c1, p1, c2, src, rcv, rcvf, srcf, acc, xb,
    tab_sem, l1_send, l1_recv, l2_send, l2_recv, rc_send, rc_recv,
    g1_send, g1_recv, g2_send, g2_recv, sib_send, sib_recv,
):
    R = lax.axis_index("rcv")
    S = lax.axis_index("seg")
    yl = R // 32
    z = (R // 2) % Z
    core = R % 2
    m = R // 8
    w = R % 8
    zr = z % 4
    zq = z // 4
    own = w == 0

    def dev(yl_, z_, core_):
        return yl_ * 32 + z_ * 2 + core_

    def along(d):
        return lax.rem(z + Z + d, Z)

    sibling = dev(yl, z, 1 - core)

    tab_copies = []
    for i in range(3):
        rows = pl.ds(512 * i, 512)
        cp = pltpu.make_async_copy(tab_hbm.at[rows], tab.at[rows], tab_sem.at[i])
        cp.start()
        tab_copies.append(cp)
    inv_copy = pltpu.make_async_copy(inv_hbm, inv, tab_sem.at[3])
    inv_copy.start()

    barrier = pltpu.get_barrier_semaphore()

    def greet(r, s):
        pl.semaphore_signal(barrier, inc=1, device_id=(r, s), device_id_type=MESH)

    for d in range(1, 8):
        greet(lax.rem(m + d, 8) * 8 + w, S)
        greet(R, lax.rem(S + d, 8))
        greet(m * 8 + lax.rem(w + d, 8), S ^ w)

    @pl.when(jnp.logical_not(own))
    def _():
        greet(R, S ^ w)

    for d in (-2, -1, 1, 2):
        for dy in (0, 1):
            greet(dev(yl ^ dy, along(d), core), S)
    greet(sibling, S)

    samples = tr_ref.shape[1]
    spec = None
    for i in range(3):
        tab_copies[i].wait()
        part = jnp.dot(
            tr_ref[:, pl.ds(512 * i, min(512, samples - 512 * i))],
            tab[pl.ds(512 * i, min(512, samples - 512 * i)), :],
            preferred_element_type=jnp.float32,
        )
        spec = part if spec is None else spec + part
    sq = spec * spec
    pa = sq[:, 0:128] + sq[:, 128:256]
    pb = sq[:, 256:384] + sq[:, 384:512]
    pe = sq[:, 512:640]
    level = jnp.sum(pa + pb + pe, axis=1, keepdims=True) * (1.0 / F) + 1e-06
    level = 0.1 * level
    pe = pe + pltpu.roll(pe, 64, 1)
    rows = lax.broadcasted_iota(jnp.int32, (64, 1), 0) // 16
    flag = jnp.zeros((64, 1), jnp.float32)
    for g in range(4):
        flag = jnp.where(rows == g, valid_ref[g].astype(jnp.float32), flag)
    fa = lax.rsqrt(pa + level)
    fb = lax.rsqrt(pb + level)
    fe = lax.rsqrt(pe + level)
    factor = jnp.concatenate([fa, fa, fb, fb, fe], axis=1)
    whitened = (spec * factor * flag).astype(jnp.bfloat16)
    for b in range(8):
        white[b] = whitened[8 * b : 8 * b + 8]

    pl.semaphore_wait(barrier, jnp.where(own, 30, 31))

    l1 = []
    for d in range(1, 8):
        other = lax.rem(m + d, 8)
        cp = pltpu.make_async_remote_copy(
            src_ref=white.at[other], dst_ref=c1.at[m],
            send_sem=l1_send.at[d], recv_sem=l1_recv.at[d],
            device_id=(other * 8 + w, S), device_id_type=MESH,
        )
        cp.start()
        l1.append(cp)
    c1[m] = white[m]

    for cp in l1:
        cp.wait_recv()
    v = lax.broadcasted_iota(jnp.int32, (8, 1), 0) + 8 * (m % 2)
    cand = [c1[mm].astype(jnp.float32) for mm in range(8)]
    for p in range(PANELS):
        st = start_ref[p]
        pick = jnp.zeros((8, C), jnp.float32)
        for mm in range(8):
            j = 128 * mm + 16 * w + v - st
            pick = jnp.where((j >= 0) & (j < SRC), cand[mm], pick)
        p1[p] = pick.astype(jnp.bfloat16)

    l2 = []
    for d in range(8):
        to = S ^ d
        cp = pltpu.make_async_remote_copy(
            src_ref=p1, dst_ref=c2.at[w],
            send_sem=l2_send.at[d], recv_sem=l2_recv.at[w],
            device_id=(m * 8 + d, to), device_id_type=MESH,
        )
        l2.append(cp)
        if d == 0:
            pl.when(jnp.logical_not(own))(cp.start)
        else:
            cp.start()

    @pl.when(own)
    def _():
        c2[w] = p1[...]

    rc = []
    for d in range(1, 8):
        cp = pltpu.make_async_remote_copy(
            src_ref=white, dst_ref=rcv.at[S],
            send_sem=rc_send.at[d], recv_sem=rc_recv.at[d],
            device_id=(R, lax.rem(S + d, 8)), device_id_type=MESH,
        )
        cp.start()
        rc.append(cp)
    rcv[S] = white[...]
    acc[...] = jnp.zeros_like(acc)

    for ww in range(8):
        cp = pltpu.make_async_remote_copy(
            src_ref=p1, dst_ref=c2.at[ww],
            send_sem=l2_send.at[0], recv_sem=l2_recv.at[ww],
            device_id=(m * 8, S), device_id_type=MESH,
        )
        if ww == 0:
            pl.when(jnp.logical_not(own))(cp.wait_recv)
        else:
            cp.wait_recv()

    for p in range(PANELS):
        st = start_ref[p]
        pick = jnp.zeros((8, C), jnp.float32)
        for ww in range(8):
            j = (16 * ww + v - st) & (SRC - 1)
            pick = jnp.where((j >> 4) == S, c2[ww, p].astype(jnp.float32), pick)
        src[yl, core, zr, zq, p] = pick.astype(jnp.bfloat16)

    g1 = []
    for d in range(1, 4):
        piece = src.at[yl, core, zr, zq]
        cp = pltpu.make_async_remote_copy(
            src_ref=piece, dst_ref=piece,
            send_sem=g1_send.at[d], recv_sem=g1_recv.at[d],
            device_id=(dev(yl, along(4 * d), core), S), device_id_type=MESH,
        )
        cp.start()
        g1.append(cp)
    for cp in g1:
        cp.wait_recv()

    g2 = []
    for i in range(1, 8):
        dz, dy = (i // 2) ^ (i // 4), i % 2
        for half in range(2):
            to = (0, -1, 2 - 4 * half, 1)[dz]
            pair = src.at[yl, core, zr, pl.ds(2 * half, 2)]
            cp = pltpu.make_async_remote_copy(
                src_ref=pair, dst_ref=pair,
                send_sem=g2_send.at[i, half], recv_sem=g2_recv.at[i, half],
                device_id=(dev(yl ^ dy, along(to), core), S), device_id_type=MESH,
            )
            cp.start()
            g2.append(cp)

    def group(i):
        k = i // 2
        return yl ^ (i % 2), lax.rem(zr + (k ^ (k // 2)), 4)

    def across(i):
        y, q = group(i)
        four = src.at[y, core, q]
        return pltpu.make_async_remote_copy(
            src_ref=four, dst_ref=four,
            send_sem=sib_send.at[i], recv_sem=sib_recv.at[i],
            device_id=(sibling, S), device_id_type=MESH,
        )

    def chunk(i, c):
        y, q = group(i)
        sbase = 4 * ((q * 2 + c) ^ S) + 2 * y
        for n in range(4):
            for p in range(PANELS):
                srcf[n, p] = src[y, c, q, n, p].astype(jnp.float32)

        def panel(p, carry):
            for vg in range(4):
                for t in range(3):
                    lanes = [pl.ds(256 * t, 128), pl.ds(256 * t + 128, 128)]
                    sums = [
                        [
                            [acc[p, vg * 4 + i, half, :, ln] for ln in lanes]
                            for half in range(2)
                        ]
                        for i in range(4)
                    ]
                    for g in range(2):
                        n = 2 * g + vg // 2
                        got = [
                            [rcvf[sbase + g, half, :, ln] for ln in lanes]
                            for half in range(2)
                        ]
                        for i in range(4):
                            row = pl.ds((vg % 2) * 4 + i, 1)
                            s0 = srcf[n, p, row, lanes[0]]
                            if t < 2:
                                s1 = srcf[n, p, row, lanes[1]]
                            for half in range(2):
                                r0, r1 = got[half]
                                here = sums[i][half]
                                if t < 2:
                                    here[0] = here[0] + s0 * r0 + s1 * r1
                                    here[1] = here[1] + s0 * r1 - s1 * r0
                                else:
                                    here[0] = here[0] + s0 * r0
                                    here[1] = here[1] + s0 * r1
                    for i in range(4):
                        for half in range(2):
                            for n in range(2):
                                acc[p, vg * 4 + i, half, :, lanes[n]] = sums[i][half][n]
            return carry

        lax.fori_loop(0, PANELS, panel, 0)

    across(0).start()
    for cp in rc:
        cp.wait_recv()

    def widen(sp, carry):
        for b in range(8):
            block = rcv[sp, b].astype(jnp.float32)
            rcvf[sp * 4 + b // 2, b % 2, :, pl.ds(0, C)] = block
            rcvf[sp * 4 + b // 2, b % 2, :, pl.ds(C, 128)] = pltpu.roll(
                block[:, 512:640], 64, 1
            )
        return carry

    lax.fori_loop(0, 8, widen, 0)
    chunk(0, core)

    def stage(i, carry):
        for half in range(2):
            pair = src.at[yl, core, zr, pl.ds(0, 2)]
            pltpu.make_async_remote_copy(
                src_ref=pair, dst_ref=pair,
                send_sem=g2_send.at[i, half], recv_sem=g2_recv.at[i, half],
                device_id=(sibling, S), device_id_type=MESH,
            ).wait_recv()
        across(i).start()
        chunk(i, core)
        across(i - 1).wait_recv()
        chunk(i - 1, 1 - core)
        return carry

    lax.fori_loop(1, 8, stage, 0)
    across(7).wait_recv()
    chunk(7, 1 - core)

    inv_copy.wait()
    for p in range(PANELS):
        st = start_ref[p]
        for i in range(16):
            xb[pl.ds(16 * i, 16)] = (
                acc[p, (st + i) & 15].reshape(16, W).astype(jnp.bfloat16)
            )
        out_ref[p] = jnp.dot(
            xb[...], inv[...], preferred_element_type=jnp.float32
        )

    for cp in l1 + rc + g1 + g2 + l2[1:]:
        cp.wait_send()
    pl.when(jnp.logical_not(own))(l2[0].wait_send)

    def drain(i, carry):
        across(i).wait_send()
        return carry

    lax.fori_loop(0, 8, drain, 0)


def body(traces, panel_start, valid):
    rows, segs, samples = traces.shape
    table = jnp.asarray(forward_table(samples))
    inv = jnp.asarray(inverse_table(segs * lax.axis_size("seg")))
    tr = jnp.transpose(traces, (1, 0, 2)).reshape(segs * rows, samples)
    bf = jnp.bfloat16
    f32 = jnp.float32
    dma = pltpu.SemaphoreType.DMA
    out = pl.pallas_call(
        kernel,
        out_shape=jax.ShapeDtypeStruct((PANELS, 256, 2 * LAG), f32),
        in_specs=[
            pl.BlockSpec(memory_space=pltpu.SMEM),
            pl.BlockSpec(memory_space=pltpu.SMEM),
            pl.BlockSpec(memory_space=pltpu.VMEM),
            pl.BlockSpec(memory_space=pl.ANY),
            pl.BlockSpec(memory_space=pl.ANY),
        ],
        out_specs=pl.BlockSpec(memory_space=pltpu.VMEM),
        scratch_shapes=[
            pltpu.VMEM((KPAD, C), bf),
            pltpu.VMEM((W, 2 * LAG), bf),
            pltpu.VMEM((8, 8, C), bf),
            pltpu.VMEM((8, 8, C), bf),
            pltpu.VMEM((2, 8, C), bf),
            pltpu.VMEM((8, 2, 8, C), bf),
            pltpu.VMEM((2, 2, 4, 4, 2, 8, C), bf),
            pltpu.VMEM((8, 8, 8, C), bf),
            pltpu.VMEM((SEGS, 2, 8, W), f32),
            pltpu.VMEM((4, 2, 8, C), f32),
            pltpu.VMEM((2, 16, 2, 8, W), f32),
            pltpu.VMEM((256, W), bf),
            dma((4,)),
            dma((8,)), dma((8,)), dma((8,)), dma((8,)), dma((8,)), dma((8,)),
            dma((4,)), dma((4,)), dma((8, 2)), dma((8, 2)), dma((8,)), dma((8,)),
        ],
        compiler_params=pltpu.CompilerParams(
            collective_id=0, has_side_effects=True, vmem_limit_bytes=60 * 1024 * 1024
        ),
    )(panel_start, valid, tr, table, inv)
    return out.reshape(PANELS, 16, 16, 2 * LAG)


def solution(mesh):
    return jax.shard_map(
        body,
        mesh=mesh,
        in_specs=(P("rcv", "seg", None), P(), P("seg")),
        out_specs=P(None, "seg", "rcv", None),
        check_vma=False,
    )
```

time: 75.4 us -> 60.7 us (0.81); the launches traced: 75.2 us -> 59.5 us
  Pallas kernels: 71.6 us -> 56 us
    pallas_call x1, Pallas kernels: 71.6 us -> 56 us  [body(): pl.pallas_call(kernel, out_shape=jax.ShapeDtypeStruct((PANELS, 256, 2 * L...]
where the time goes in v2:
time: 60.7 us; the launch traced here: 59.5 us
  Pallas kernels  56 us (92%)
  local copies, waits for them, and re-layouts  3.51 us (6%)
    pallas_call x1, Pallas kernels, body(): pl.pallas_call(kernel, out_shape=jax.ShapeDtypeStruct((PANELS, 256, 2 * L...  56 us
    unnamed x1, local copies, waits for them, and re-layouts  1.87 us
    transpose x1, local copies, waits for them, and re-layouts, body(): tr = jnp.transpose(traces, (1, 0, 2)).reshape(segs * rows, samples)  1.64 us

profile of v2, /device:TPU:1, one launch (start us, length us, event | category | flops | bytes accessed | tf_op | source)
XLA Modules:
  0.0 59.5 jit_solution(15877774380227922574)
XLA Ops:
  0.0 1.6 %copy.6 = bf16[4,16,1500]{2,1,0:T(8,128)(2,1)} copy(bf16[4,16,1500]{2,0,1:T(4,128)(2,1)} %bitcast.5) | data formatting | bytes 384000 | tf_op jit(solution)/shard_map/transpose | solution.py:362
  1.6 56.0 %shard_map.55 = f32[2,256,256]{2,1,0:T(8,128)} custom-call(s32[2]{0:T(128)} %start_ref.1, s32[4]{0:T(128)} %valid_ref.1, bf16[64,1500]{1,0:T(8,128)(2,1)} %bitcast.4, bf16[1536,640]{1,0:T(8,128)(2,1)} %constant.4.clone.tab_hbm, bf16[768,256]{1,0:T(8,128)(2,1)} %constant.5.clone.inv_hbm), custom_call_target="tpu_custom_call" | custom-call | tf_op jit(solution)/shard_map/pallas_call | solution.py:366
  57.6 1.9 %copy.8 = f32[2,16,16,256]{3,2,1,0:T(8,128)} copy(f32[2,16,16,256]{3,2,1,0:T(8,128)} %bitcast.3) | data formatting | bytes 1048576

commit v3 on v2

--- a/solution.py
+++ b/solution.py
@@ -57,8 +57,8 @@
 
 
 def kernel(
-    start_ref, valid_ref, tr_ref, tab_hbm, inv_hbm, out_ref,
-    tab, inv, white, c1, p1, c2, src, rcv, rcvf, srcf, acc, xb,
+    start_ref, valid_ref, tr_hbm, tab_hbm, out_ref,
+    tr, tab, inv, white, c1, p1, c2, src, rcv, rcvf, srcf, acc, xb,
     tab_sem, l1_send, l1_recv, l2_send, l2_recv, rc_send, rc_recv,
     g1_send, g1_recv, g2_send, g2_recv, sib_send, sib_recv,
 ):
@@ -81,23 +81,26 @@
 
     sibling = dev(yl, z, 1 - core)
 
+    barrier = pltpu.get_barrier_semaphore()
+
+    def greet(r, s):
+        pl.semaphore_signal(barrier, inc=1, device_id=(r, s), device_id_type=MESH)
+
+    for d in (2, 6, 1, 3, 5, 7, 4):
+        greet(lax.rem(m + d, 8) * 8 + w, S)
+    tr_copy = pltpu.make_async_copy(tr_hbm, tr, tab_sem.at[4])
+    tr_copy.start()
     tab_copies = []
     for i in range(3):
         rows = pl.ds(512 * i, 512)
         cp = pltpu.make_async_copy(tab_hbm.at[rows], tab.at[rows], tab_sem.at[i])
         cp.start()
         tab_copies.append(cp)
-    inv_copy = pltpu.make_async_copy(inv_hbm, inv, tab_sem.at[3])
+    inv_copy = pltpu.make_async_copy(
+        tab_hbm.at[pl.ds(KPAD, W), pl.ds(0, 2 * LAG)], inv, tab_sem.at[3]
+    )
     inv_copy.start()
-
-    barrier = pltpu.get_barrier_semaphore()
-
-    def greet(r, s):
-        pl.semaphore_signal(barrier, inc=1, device_id=(r, s), device_id_type=MESH)
-
     for d in range(1, 8):
-        greet(lax.rem(m + d, 8) * 8 + w, S)
-        greet(R, lax.rem(S + d, 8))
         greet(m * 8 + lax.rem(w + d, 8), S ^ w)
 
     @pl.when(jnp.logical_not(own))
@@ -108,13 +111,22 @@
         for dy in (0, 1):
             greet(dev(yl ^ dy, along(d), core), S)
     greet(sibling, S)
-
-    samples = tr_ref.shape[1]
+    for d in range(1, 8):
+        greet(R, lax.rem(S + d, 8))
+
+    acc[...] = jnp.zeros_like(acc)
+
+    tr_copy.wait()
+    samples = tr.shape[2]
+    wide = tr[...].astype(jnp.float32)
+    rows = jnp.concatenate(
+        [wide[:, g, :].astype(jnp.bfloat16) for g in range(4)], axis=0
+    )
     spec = None
     for i in range(3):
         tab_copies[i].wait()
         part = jnp.dot(
-            tr_ref[:, pl.ds(512 * i, min(512, samples - 512 * i))],
+            rows[:, 512 * i : min(512 * i + 512, samples)],
             tab[pl.ds(512 * i, min(512, samples - 512 * i)), :],
             preferred_element_type=jnp.float32,
         )
@@ -141,7 +153,7 @@
     pl.semaphore_wait(barrier, jnp.where(own, 30, 31))
 
     l1 = []
-    for d in range(1, 8):
+    for d in (2, 6, 1, 3, 5, 7, 4):
         other = lax.rem(m + d, 8)
         cp = pltpu.make_async_remote_copy(
             src_ref=white.at[other], dst_ref=c1.at[m],
@@ -151,6 +163,17 @@
         cp.start()
         l1.append(cp)
     c1[m] = white[m]
+
+    rc = []
+    for d in range(1, 8):
+        cp = pltpu.make_async_remote_copy(
+            src_ref=white, dst_ref=rcv.at[S],
+            send_sem=rc_send.at[d], recv_sem=rc_recv.at[d],
+            device_id=(R, lax.rem(S + d, 8)), device_id_type=MESH,
+        )
+        cp.start()
+        rc.append(cp)
+    rcv[S] = white[...]
 
     for cp in l1:
         cp.wait_recv()
@@ -182,18 +205,6 @@
     def _():
         c2[w] = p1[...]
 
-    rc = []
-    for d in range(1, 8):
-        cp = pltpu.make_async_remote_copy(
-            src_ref=white, dst_ref=rcv.at[S],
-            send_sem=rc_send.at[d], recv_sem=rc_recv.at[d],
-            device_id=(R, lax.rem(S + d, 8)), device_id_type=MESH,
-        )
-        cp.start()
-        rc.append(cp)
-    rcv[S] = white[...]
-    acc[...] = jnp.zeros_like(acc)
-
     for ww in range(8):
         cp = pltpu.make_async_remote_copy(
             src_ref=p1, dst_ref=c2.at[ww],
@@ -213,52 +224,76 @@
             pick = jnp.where((j >> 4) == S, c2[ww, p].astype(jnp.float32), pick)
         src[yl, core, zr, zq, p] = pick.astype(jnp.bfloat16)
 
-    g1 = []
-    for d in range(1, 4):
+    near = zq // 2
+    far = 1 - near
+    g1 = {}
+    for x in (2, 1, 3):
         piece = src.at[yl, core, zr, zq]
-        cp = pltpu.make_async_remote_copy(
+        g1[x] = pltpu.make_async_remote_copy(
             src_ref=piece, dst_ref=piece,
-            send_sem=g1_send.at[d], recv_sem=g1_recv.at[d],
-            device_id=(dev(yl, along(4 * d), core), S), device_id_type=MESH,
-        )
-        cp.start()
-        g1.append(cp)
-    for cp in g1:
-        cp.wait_recv()
-
-    g2 = []
-    for i in range(1, 8):
-        dz, dy = (i // 2) ^ (i // 4), i % 2
-        for half in range(2):
-            to = (0, -1, 2 - 4 * half, 1)[dz]
-            pair = src.at[yl, core, zr, pl.ds(2 * half, 2)]
-            cp = pltpu.make_async_remote_copy(
-                src_ref=pair, dst_ref=pair,
-                send_sem=g2_send.at[i, half], recv_sem=g2_recv.at[i, half],
-                device_id=(dev(yl ^ dy, along(to), core), S), device_id_type=MESH,
-            )
-            cp.start()
-            g2.append(cp)
+            send_sem=g1_send.at[x], recv_sem=g1_recv.at[x],
+            device_id=(dev(yl, (zq ^ x) * 4 + zr, core), S), device_id_type=MESH,
+        )
+        g1[x].start()
 
     def group(i):
         k = i // 2
         return yl ^ (i % 2), lax.rem(zr + (k ^ (k // 2)), 4)
 
-    def across(i):
+    def pair(i, half, c):
         y, q = group(i)
-        four = src.at[y, core, q]
+        return src.at[y, c, q, pl.ds(2 * half, 2)]
+
+    def window(i, half):
+        dz, dy = (i // 2) ^ (i // 4), i % 2
+        to = (0, -1, 2 - 4 * half, 1)[dz]
         return pltpu.make_async_remote_copy(
-            src_ref=four, dst_ref=four,
-            send_sem=sib_send.at[i], recv_sem=sib_recv.at[i],
+            src_ref=pair(0, half, core), dst_ref=pair(0, half, core),
+            send_sem=g2_send.at[i, half], recv_sem=g2_recv.at[i, half],
+            device_id=(dev(yl ^ dy, along(to), core), S), device_id_type=MESH,
+        )
+
+    def across(i, half):
+        return pltpu.make_async_remote_copy(
+            src_ref=pair(i, half, core), dst_ref=pair(i, half, core),
+            send_sem=sib_send.at[i, half], recv_sem=sib_recv.at[i, half],
             device_id=(sibling, S), device_id_type=MESH,
         )
 
-    def chunk(i, c):
-        y, q = group(i)
-        sbase = 4 * ((q * 2 + c) ^ S) + 2 * y
-        for n in range(4):
-            for p in range(PANELS):
-                srcf[n, p] = src[y, c, q, n, p].astype(jnp.float32)
+    g1[1].wait_recv()
+    for i in range(1, 8):
+        window(i, near).start()
+    across(0, near).start()
+    g1[3].wait_recv()
+    g1[2].wait_recv()
+    for i in range(1, 8):
+        window(i, far).start()
+    across(0, far).start()
+
+    for cp in rc:
+        cp.wait_recv()
+
+    def widen(sp, carry):
+        for b in range(8):
+            block = rcv[sp, b].astype(jnp.float32)
+            rcvf[sp * 4 + b // 2, b % 2, :, pl.ds(0, C)] = block
+            rcvf[sp * 4 + b // 2, b % 2, :, pl.ds(C, 128)] = pltpu.roll(
+                block[:, 512:640], 64, 1
+            )
+        return carry
+
+    lax.fori_loop(0, 8, widen, 0)
+
+    def chunk(*parts):
+        segs = []
+        for g, (i, half, c) in enumerate(parts):
+            y, q = group(i)
+            segs.append(4 * ((q * 2 + c) ^ S) + 2 * y + half)
+            for n in range(2):
+                for p in range(PANELS):
+                    srcf[2 * g + n, p] = src[y, c, q, 2 * half + n, p].astype(
+                        jnp.float32
+                    )
 
         def panel(p, carry):
             for vg in range(4):
@@ -274,7 +309,7 @@
                     for g in range(2):
                         n = 2 * g + vg // 2
                         got = [
-                            [rcvf[sbase + g, half, :, ln] for ln in lanes]
+                            [rcvf[segs[g], half, :, ln] for ln in lanes]
                             for half in range(2)
                         ]
                         for i in range(4):
@@ -299,39 +334,47 @@
 
         lax.fori_loop(0, PANELS, panel, 0)
 
-    across(0).start()
-    for cp in rc:
-        cp.wait_recv()
-
-    def widen(sp, carry):
-        for b in range(8):
-            block = rcv[sp, b].astype(jnp.float32)
-            rcvf[sp * 4 + b // 2, b % 2, :, pl.ds(0, C)] = block
-            rcvf[sp * 4 + b // 2, b % 2, :, pl.ds(C, 128)] = pltpu.roll(
-                block[:, 512:640], 64, 1
-            )
+    def half_of(j):
+        return jnp.where(j < 8, near, far)
+
+    def arrived(i, half):
+        ref = pair(0, near, core)
+        return pltpu.make_async_remote_copy(
+            src_ref=ref, dst_ref=ref,
+            send_sem=g2_send.at[i, half], recv_sem=g2_recv.at[i, half],
+            device_id=(sibling, S), device_id_type=MESH,
+        )
+
+    def take(j):
+        i, half = j % 8, half_of(j)
+
+        @pl.when(i > 0)
+        def _():
+            arrived(i, half).wait_recv()
+            across(i, half).start()
+
+        return i, half, core
+
+    def given(j):
+        i, half = j % 8, half_of(j)
+        across(i, half).wait_recv()
+        return i, half, 1 - core
+
+    def first(t, carry):
+        chunk(take(2 * t), take(2 * t + 1))
         return carry
 
-    lax.fori_loop(0, 8, widen, 0)
-    chunk(0, core)
-
-    def stage(i, carry):
-        for half in range(2):
-            pair = src.at[yl, core, zr, pl.ds(0, 2)]
-            pltpu.make_async_remote_copy(
-                src_ref=pair, dst_ref=pair,
-                send_sem=g2_send.at[i, half], recv_sem=g2_recv.at[i, half],
-                device_id=(sibling, S), device_id_type=MESH,
-            ).wait_recv()
-        across(i).start()
-        chunk(i, core)
-        across(i - 1).wait_recv()
-        chunk(i - 1, 1 - core)
+    def middle(j, carry):
+        chunk(take(j), given(j - 4))
         return carry
 
-    lax.fori_loop(1, 8, stage, 0)
-    across(7).wait_recv()
-    chunk(7, 1 - core)
+    def final(t, carry):
+        chunk(given(2 * t), given(2 * t + 1))
+        return carry
+
+    lax.fori_loop(0, 2, first, 0)
+    lax.fori_loop(4, 16, middle, 0)
+    lax.fori_loop(6, 8, final, 0)
 
     inv_copy.wait()
     for p in range(PANELS):
@@ -344,22 +387,28 @@
             xb[...], inv[...], preferred_element_type=jnp.float32
         )
 
-    for cp in l1 + rc + g1 + g2 + l2[1:]:
+    for cp in l1 + rc + [g1[1], g1[2], g1[3]] + l2[1:]:
         cp.wait_send()
     pl.when(jnp.logical_not(own))(l2[0].wait_send)
 
-    def drain(i, carry):
-        across(i).wait_send()
+    def drain(j, carry):
+        i, half = j % 8, half_of(j)
+        across(i, half).wait_send()
+
+        @pl.when(i > 0)
+        def _():
+            arrived(i, half).wait_send()
+
         return carry
 
-    lax.fori_loop(0, 8, drain, 0)
+    lax.fori_loop(0, 16, drain, 0)
 
 
 def body(traces, panel_start, valid):
     rows, segs, samples = traces.shape
-    table = jnp.asarray(forward_table(samples))
-    inv = jnp.asarray(inverse_table(segs * lax.axis_size("seg")))
-    tr = jnp.transpose(traces, (1, 0, 2)).reshape(segs * rows, samples)
+    tables = np.zeros((KPAD + W, C), ml_dtypes.bfloat16)
+    tables[:KPAD] = forward_table(samples)
+    tables[KPAD:, : 2 * LAG] = inverse_table(segs * lax.axis_size("seg"))
     bf = jnp.bfloat16
     f32 = jnp.float32
     dma = pltpu.SemaphoreType.DMA
@@ -369,12 +418,12 @@
         in_specs=[
             pl.BlockSpec(memory_space=pltpu.SMEM),
             pl.BlockSpec(memory_space=pltpu.SMEM),
-            pl.BlockSpec(memory_space=pltpu.VMEM),
             pl.BlockSpec(memory_space=pl.ANY),
             pl.BlockSpec(memory_space=pl.ANY),
         ],
         out_specs=pl.BlockSpec(memory_space=pltpu.VMEM),
         scratch_shapes=[
+            pltpu.VMEM((rows, segs, samples), bf),
             pltpu.VMEM((KPAD, C), bf),
             pltpu.VMEM((W, 2 * LAG), bf),
             pltpu.VMEM((8, 8, C), bf),
@@ -387,14 +436,14 @@
             pltpu.VMEM((4, 2, 8, C), f32),
             pltpu.VMEM((2, 16, 2, 8, W), f32),
             pltpu.VMEM((256, W), bf),
-            dma((4,)),
+            dma((5,)),
             dma((8,)), dma((8,)), dma((8,)), dma((8,)), dma((8,)), dma((8,)),
-            dma((4,)), dma((4,)), dma((8, 2)), dma((8, 2)), dma((8,)), dma((8,)),
+            dma((4,)), dma((4,)), dma((8, 2)), dma((8, 2)), dma((8, 2)), dma((8, 2)),
         ],
         compiler_params=pltpu.CompilerParams(
-            collective_id=0, has_side_effects=True, vmem_limit_bytes=60 * 1024 * 1024
+            collective_id=0, has_side_effects=True, vmem_limit_bytes=62 * 1024 * 1024
         ),
-    )(panel_start, valid, tr, table, inv)
+    )(panel_start, valid, traces, jnp.asarray(tables))
     return out.reshape(PANELS, 16, 16, 2 * LAG)
 
 

time: 60.7 us -> 59.4 us (0.979); the launches traced: 59.5 us -> 59.2 us
  local copies, waits for them, and re-layouts: 3.51 us -> 1.87 us
  Pallas kernels: 56 us -> 57.3 us
    transpose x1 -> x0, local copies, waits for them, and re-layouts: 1.64 us -> none  [body(): tr = jnp.transpose(traces, (1, 0, 2)).reshape(segs * rows, samples)]
    pallas_call x1, Pallas kernels: 56 us -> 57.3 us  [body(): pl.pallas_call(kernel, out_shape=jax.ShapeDtypeStruct((PANELS, 256, 2 * L...]
where the time goes in v3:
time: 59.4 us; the launch traced here: 59.2 us
  Pallas kernels  57.3 us (96%)
  local copies, waits for them, and re-layouts  1.87 us (3%)
    pallas_call x1, Pallas kernels, body(): pl.pallas_call(kernel, out_shape=jax.ShapeDtypeStruct((PANELS, 256, 2 * L...  57.3 us
    unnamed x1, local copies, waits for them, and re-layouts  1.87 us

profile of v3, /device:TPU:1, one launch (start us, length us, event | category | flops | bytes accessed | tf_op | source)
XLA Modules:
  0.0 59.2 jit_solution(3268812151152197466)
XLA Ops:
  0.0 57.3 %shard_map.46 = f32[2,256,256]{2,1,0:T(8,128)} custom-call(s32[2]{0:T(128)} %start_ref.1, s32[4]{0:T(128)} %valid_ref.1, bf16[16,4,1500]{2,1,0:T(4,128)(2,1)} %tr_hbm.1, bf16[2304,640]{1,0:T(8,128)(2,1)} %constant.2.clone.tab_hbm), custom_call_target="tpu_custom_call" | custom-call | tf_op jit(solution)/shard_map/pallas_call | solution.py:415
  57.3 1.9 %copy.6 = f32[2,16,16,256]{3,2,1,0:T(8,128)} copy(f32[2,16,16,256]{3,2,1,0:T(8,128)} %bitcast.1) | data formatting | bytes 1048576

commit v4 on v3

--- a/solution.py
+++ b/solution.py
@@ -43,14 +43,13 @@
     return full.astype(ml_dtypes.bfloat16)
 
 
-def inverse_table(total_segs):
+def inverse_table():
     freqs = K0 + np.arange(F, dtype=np.int64)
     delays = np.arange(2 * LAG, dtype=np.int64) - LAG
     phase = np.mod(freqs[:, None] * delays[None, :], NFFT)
     angle = 2.0 * math.pi / NFFT * phase
-    scale = 1.0 / math.sqrt(F) / math.sqrt(total_segs)
-    cos = np.cos(angle) * scale
-    sin = np.sin(angle) * scale
+    cos = np.cos(angle)
+    sin = np.sin(angle)
     rows = [cos[:128], -sin[:128], cos[128:256], -sin[128:256]]
     rows += [cos[256:], cos[256:], -sin[256:], sin[256:]]
     return np.concatenate(rows, axis=0).astype(np.float32).astype(ml_dtypes.bfloat16)
@@ -408,7 +407,7 @@
     rows, segs, samples = traces.shape
     tables = np.zeros((KPAD + W, C), ml_dtypes.bfloat16)
     tables[:KPAD] = forward_table(samples)
-    tables[KPAD:, : 2 * LAG] = inverse_table(segs * lax.axis_size("seg"))
+    tables[KPAD:, : 2 * LAG] = inverse_table()
     bf = jnp.bfloat16
     f32 = jnp.float32
     dma = pltpu.SemaphoreType.DMA
@@ -444,6 +443,8 @@
             collective_id=0, has_side_effects=True, vmem_limit_bytes=62 * 1024 * 1024
         ),
     )(panel_start, valid, traces, jnp.asarray(tables))
+    total_segs = segs * lax.axis_size("seg")
+    out = out * (1.0 / math.sqrt(F * total_segs))
     return out.reshape(PANELS, 16, 16, 2 * LAG)
 
 

time: 59.4 us -> 59.4 us (level)
  other arithmetic: 0 us -> 1.88 us
  local copies, waits for them, and re-layouts: 1.87 us -> 0 us
    mul x0 -> x1, other arithmetic: none -> 1.88 us  [body(): out = out * (1.0 / math.sqrt(F * total_segs))]
    unnamed x1 -> x0, local copies, waits for them, and re-layouts: 1.87 us -> none
where the time goes in v4:
time: 59.4 us; the launch traced here: 59.2 us
  Pallas kernels  57.3 us (96%)
  other arithmetic  1.88 us (3%)
    pallas_call x1, Pallas kernels, body(): pl.pallas_call(kernel, out_shape=jax.ShapeDtypeStruct((PANELS, 256, 2 * L...  57.3 us
    mul x1, other arithmetic, body(): out = out * (1.0 / math.sqrt(F * total_segs))  1.88 us

profile of v4, /device:TPU:1, one launch (start us, length us, event | category | flops | bytes accessed | tf_op | source)
XLA Modules:
  0.0 59.2 jit_solution(3620396525830937332)
XLA Ops:
  0.0 57.3 %shard_map.46 = f32[2,256,256]{2,1,0:T(8,128)} custom-call(s32[2]{0:T(128)} %start_ref.1, s32[4]{0:T(128)} %valid_ref.1, bf16[16,4,1500]{2,1,0:T(4,128)(2,1)} %tr_hbm.1, bf16[2304,640]{1,0:T(8,128)(2,1)} %constant.4.clone.tab_hbm), custom_call_target="tpu_custom_call" | custom-call | tf_op jit(solution)/shard_map/pallas_call | solution.py:414
  57.3 1.9 %broadcast_multiply_fusion = f32[2,256,256]{2,1,0:T(8,128)} fusion(f32[2,256,256]{2,1,0:T(8,128)} %shard_map.46), kind=kLoop, calls=%fused_computation | loop fusion | flops 131072 | bytes 1048576 | tf_op jit(solution)/shard_map/mul | solution.py:447

commit v5 on v4

--- a/solution.py
+++ b/solution.py
@@ -243,11 +243,11 @@
         y, q = group(i)
         return src.at[y, c, q, pl.ds(2 * half, 2)]
 
-    def window(i, half):
+    def window(i, half, ref):
         dz, dy = (i // 2) ^ (i // 4), i % 2
         to = (0, -1, 2 - 4 * half, 1)[dz]
         return pltpu.make_async_remote_copy(
-            src_ref=pair(0, half, core), dst_ref=pair(0, half, core),
+            src_ref=ref, dst_ref=ref,
             send_sem=g2_send.at[i, half], recv_sem=g2_recv.at[i, half],
             device_id=(dev(yl ^ dy, along(to), core), S), device_id_type=MESH,
         )
@@ -259,14 +259,16 @@
             device_id=(sibling, S), device_id_type=MESH,
         )
 
+    for i in range(1, 8):
+        window(i, near, src.at[yl, core, zr, zq]).start()
     g1[1].wait_recv()
     for i in range(1, 8):
-        window(i, near).start()
+        window(i, near, src.at[yl, core, zr, zq ^ 1]).start()
     across(0, near).start()
     g1[3].wait_recv()
     g1[2].wait_recv()
     for i in range(1, 8):
-        window(i, far).start()
+        window(i, far, pair(0, far, core)).start()
     across(0, far).start()
 
     for cp in rc:

time: 59.4 us -> 58.5 us (0.985)
  Pallas kernels: 57.3 us -> 56.4 us
    pallas_call x1, Pallas kernels: 57.3 us -> 56.4 us  [body(): pl.pallas_call(kernel, out_shape=jax.ShapeDtypeStruct((PANELS, 256, 2 * L...]
where the time goes in v5:
time: 58.5 us; the launch traced here: 58.3 us
  Pallas kernels  56.4 us (96%)
  other arithmetic  1.88 us (3%)
    pallas_call x1, Pallas kernels, body(): pl.pallas_call(kernel, out_shape=jax.ShapeDtypeStruct((PANELS, 256, 2 * L...  56.4 us
    mul x1, other arithmetic, body(): out = out * (1.0 / math.sqrt(F * total_segs))  1.88 us

profile of v5, /device:TPU:1, one launch (start us, length us, event | category | flops | bytes accessed | tf_op | source)
XLA Modules:
  0.0 58.3 jit_solution(14680437826185611601)
XLA Ops:
  0.0 56.4 %shard_map.46 = f32[2,256,256]{2,1,0:T(8,128)} custom-call(s32[2]{0:T(128)} %start_ref.1, s32[4]{0:T(128)} %valid_ref.1, bf16[16,4,1500]{2,1,0:T(4,128)(2,1)} %tr_hbm.1, bf16[2304,640]{1,0:T(8,128)(2,1)} %constant.4.clone.tab_hbm), custom_call_target="tpu_custom_call" | custom-call | tf_op jit(solution)/shard_map/pallas_call | solution.py:416
  56.4 1.9 %broadcast_multiply_fusion = f32[2,256,256]{2,1,0:T(8,128)} fusion(f32[2,256,256]{2,1,0:T(8,128)} %shard_map.46), kind=kLoop, calls=%fused_computation | loop fusion | flops 131072 | bytes 1048576 | tf_op jit(solution)/shard_map/mul | solution.py:449

commit v6 on v5

--- a/solution.py
+++ b/solution.py
@@ -265,10 +265,10 @@
     for i in range(1, 8):
         window(i, near, src.at[yl, core, zr, zq ^ 1]).start()
     across(0, near).start()
-    g1[3].wait_recv()
-    g1[2].wait_recv()
-    for i in range(1, 8):
-        window(i, far, pair(0, far, core)).start()
+    for x in (3, 2):
+        g1[x].wait_recv()
+        for i in range(1, 8):
+            window(i, far, src.at[yl, core, zr, zq ^ x]).start()
     across(0, far).start()
 
     for cp in rc:

time: 58.5 us -> 58.2 us (level)
  no operation moved by 1% of the time
where the time goes in v6:
time: 58.2 us; the launch traced here: 58 us
  Pallas kernels  56.1 us (96%)
  other arithmetic  1.88 us (3%)
    pallas_call x1, Pallas kernels, body(): pl.pallas_call(kernel, out_shape=jax.ShapeDtypeStruct((PANELS, 256, 2 * L...  56.1 us
    mul x1, other arithmetic, body(): out = out * (1.0 / math.sqrt(F * total_segs))  1.88 us

profile of v6, /device:TPU:1, one launch (start us, length us, event | category | flops | bytes accessed | tf_op | source)
XLA Modules:
  0.0 58.0 jit_solution(5268622479259278202)
XLA Ops:
  0.0 56.1 %shard_map.46 = f32[2,256,256]{2,1,0:T(8,128)} custom-call(s32[2]{0:T(128)} %start_ref.1, s32[4]{0:T(128)} %valid_ref.1, bf16[16,4,1500]{2,1,0:T(4,128)(2,1)} %tr_hbm.1, bf16[2304,640]{1,0:T(8,128)(2,1)} %constant.4.clone.tab_hbm), custom_call_target="tpu_custom_call" | custom-call | tf_op jit(solution)/shard_map/pallas_call | solution.py:416
  56.1 1.9 %broadcast_multiply_fusion = f32[2,256,256]{2,1,0:T(8,128)} fusion(f32[2,256,256]{2,1,0:T(8,128)} %shard_map.46), kind=kLoop, calls=%fused_computation | loop fusion | flops 131072 | bytes 1048576 | tf_op jit(solution)/shard_map/mul | solution.py:449
